TPU v7x, 512 devices: a whole 4x4x16 slice. The times are simulated.
512 devices in a mesh: ctx: 64 (over z_hi, y, x, core), head: 8 (over z_lo).
Axes of the slice: x: 4, y: 4, z: 16 (z_hi: 2, z_lo: 8; z = z_hi * 8 + z_lo), core: 2. Of those that a mesh axis runs over, the one named last changes fastest.
Arguments:
- queries: bfloat16 [4096, 8192], P('ctx', 'head'), may hold values from -7 to 7
- suffix_key_rows: bfloat16 [4096, 1024], P('ctx', 'head'), may hold values from -6 to 6
- suffix_value_rows: bfloat16 [4096, 1024], P('ctx', 'head'), may hold values from -6 to 6
- prefix_key_slots: bfloat16 [20480, 1024], P('ctx', 'head'), may hold values from -6 to 6
- prefix_value_slots: bfloat16 [20480, 1024], P('ctx', 'head'), may hold values from -6 to 6
- pool_counts: int32 [64], replicated, may hold values from 1 to 320, 10240 in all
- span_order: int32 [64], replicated, may hold values from 0 to 63, each once
Outputs:
- context: bfloat16 [4096, 8192], P(('ctx', 'head'))
Inputs may be any that keep to these rules, and one draw needn't show every extreme that they name: `pool_counts`: positive; the counts sum to 10240 and the largest is 320. `span_order`: each block number once.
All inputs are finite; a program needn't handle non-finite values.
Results may differ from a plain program's by a relative error of at most 0.01.
Values may be sent and summed in bfloat16 or wider, within the bound.
A program may use at most 64 MiB of HBM per device.

v0:
```python
import math

import jax
import jax.numpy as jnp
from jax import lax
from jax.sharding import PartitionSpec as P

QUERY_HEADS = 64
KEY_HEADS = 8
HEAD_SIZE = 128


hidden_mark = 1073741824


def per_device(
    queries,
    suffix_key_rows,
    suffix_value_rows,
    prefix_key_slots,
    prefix_value_slots,
    pool_counts,
    span_order,
):
    groups = lax.axis_size("ctx")
    myself = lax.axis_index("ctx")
    suf = queries.shape[0]
    pool_dev = prefix_key_slots.shape[0]
    local_kv = suffix_key_rows.shape[1] // HEAD_SIZE
    query_group = QUERY_HEADS // KEY_HEADS
    scale = 1.0 / math.sqrt(HEAD_SIZE)
    query_heads = queries.reshape(suf, local_kv, query_group, HEAD_SIZE)
    table = jnp.arange(groups, dtype=jnp.int32)
    own_span = jnp.sum(jnp.where(table == myself, span_order, 0))
    qpos = own_span * suf + jnp.arange(suf, dtype=jnp.int32)

    def lookup(value_rows, owner):
        return jnp.sum(jnp.where(owner[:, None] == table[None, :], value_rows[None, :], 0), axis=1)

    def update(carry, key_rows, value_rows, kpos):
        top, total, acc = carry
        rows = key_rows.shape[0]
        kb = key_rows.reshape(rows, local_kv, HEAD_SIZE)
        vb = value_rows.reshape(rows, local_kv, HEAD_SIZE)
        s = (
            jnp.einsum("skgd,pkd->kgsp", query_heads, kb, preferred_element_type=jnp.float32)
            * scale
        )
        mask = (kpos[None, :] <= qpos[:, None])[None, None]
        s = jnp.where(mask, s, -1e30)
        new_top = jnp.maximum(top, jnp.max(s, axis=-1))
        p = jnp.where(mask, jnp.exp(s - new_top[..., None]), 0.0)
        factor = jnp.exp(top - new_top)
        total = total * factor + jnp.sum(p, axis=-1)
        term = jnp.einsum(
            "kgsp,pkd->kgsd", p.astype(jnp.bfloat16), vb, preferred_element_type=jnp.float32
        )
        return (new_top, total, acc * factor[..., None] + term)

    def absorb(carry, key_rows, value_rows, kpos):
        rows = key_rows.shape[0]
        block = math.gcd(rows, 512)
        count = rows // block

        def step(state, inner):
            kb, vb, pb = inner
            state = update(state, kb, vb, pb)
            return (state, None)

        carry, unused = lax.scan(
            step,
            carry,
            (
                key_rows.reshape(count, block, key_rows.shape[1]),
                value_rows.reshape(count, block, value_rows.shape[1]),
                kpos.reshape(count, block),
            ),
        )
        return carry

    start_carry = (
        jnp.full((local_kv, query_group, suf), -1e30, jnp.float32),
        jnp.zeros((local_kv, query_group, suf), jnp.float32),
        jnp.zeros((local_kv, query_group, suf, HEAD_SIZE), jnp.float32),
    )
    key_rows = lax.all_gather(prefix_key_slots, "ctx", axis=0, tiled=True)
    value_rows = lax.all_gather(prefix_value_slots, "ctx", axis=0, tiled=True)
    index_rows = jnp.arange(key_rows.shape[0], dtype=jnp.int32)
    carry = absorb(
        start_carry,
        key_rows,
        value_rows,
        jnp.where(
            index_rows % pool_dev < lookup(pool_counts, index_rows // pool_dev), -1, hidden_mark
        ).astype(jnp.int32),
    )
    key_rows = lax.all_gather(suffix_key_rows, "ctx", axis=0, tiled=True)
    value_rows = lax.all_gather(suffix_value_rows, "ctx", axis=0, tiled=True)
    index_rows = jnp.arange(key_rows.shape[0], dtype=jnp.int32)
    carry = absorb(
        carry, key_rows, value_rows, lookup(span_order, index_rows // suf) * suf + index_rows % suf
    )
    top, total, acc = carry
    output = (acc / total[..., None]).astype(jnp.bfloat16)
    output = output.transpose(2, 0, 1, 3).reshape(suf, local_kv * query_group * HEAD_SIZE)
    return lax.all_to_all(output, "head", split_axis=0, concat_axis=1, tiled=True)


def solution(mesh):
    placed = (
        P("ctx", "head"),
        P("ctx", "head"),
        P("ctx", "head"),
        P("ctx", "head"),
        P("ctx", "head"),
        P(),
        P(),
    )
    return jax.shard_map(
        per_device, mesh=mesh, in_specs=placed, out_specs=P(("ctx", "head"), None), check_vma=False
    )
```

profile of v0, /device:TPU:6, one launch (start us, length us, event | category | flops | bytes accessed | tf_op | source)
XLA Modules:
  0.0 535.8 jit_solution(17359836283792536653)
XLA Ops:
  10.3 1.6 select_reduce_fusion
  12.0 1.4 fusion.56
  14.9 142.2 %all-gather.5.cloned.1.call-done = bf16[20480,128]{1,0:T(8,128)(2,1)} async-done(((bf16[320,128]{1,0:T(8,128)(2,1)}), bf16[20480,128]{1,0:T(8,128)(2,1)}) %all-gather.5.cloned.1.call-update) | async-done | bytes 5242896 | tf_op jit(solution)/shard_map/all_gather | solution.py:86
  157.1 136.8 %all-gather.7.cloned.1.call-done = bf16[20480,128]{1,0:T(8,128)(2,1)} async-done(((bf16[320,128]{1,0:T(8,128)(2,1)}), bf16[20480,128]{1,0:T(8,128)(2,1)}) %all-gather.7.cloned.1.call-update) | async-done | bytes 5242896 | tf_op jit(solution)/shard_map/all_gather | solution.py:87
  293.9 124.5 %while.31 = (s32[]{:T(128)}, f32[1,8,64]{2,1,0:T(8,128)S(1)}, f32[1,8,64]{2,1,0:T(8,128)S(1)}, f32[1,8,64,128]{3,2,1,0:T(8,128)S(1)}, s32[40,512]{1,0:T(8,128)S(...) while((s32[]{:T(128)}, f32[1,8,64]{2,1,0:T(8,128)S(1)}, ...), condition=%wide.region_5.6_spmd.clone, body=%wide.region_2.5_spmd.clone.sunk | while | flops 136809536 | bytes 4234881 | solution.py:70
  306.4 1.3 fusion.79
  322.0 1.3 fusion.79
  340.7 1.3 fusion.79
  346.9 1.3 fusion.79
  353.1 1.3 fusion.79
  362.5 1.3 fusion.79
  365.6 1.3 fusion.79
  368.7 1.3 fusion.79
  381.1 1.3 fusion.79
  406.0 1.3 fusion.79
  418.4 70.0 %all-gather.11.cloned.1.call-done = bf16[4096,128]{1,0:T(8,128)(2,1)} async-done(((bf16[64,128]{1,0:T(8,128)(2,1)}), bf16[4096,128]{1,0:T(8,128)(2,1)}) %all-gather.11.cloned.1.call-update) | async-done | bytes 1048592 | tf_op jit(solution)/shard_map/all_gather | solution.py:98
  488.3 24.9 %while.30 = (s32[]{:T(128)}, f32[1,8,64]{2,1,0:T(8,128)S(1)}, f32[1,8,64]{2,1,0:T(8,128)S(1)}, f32[1,8,64,128]{3,2,1,0:T(8,128)S(1)}, s32[8,512]{1,0:T(8,128)S(1...) while((s32[]{:T(128)}, f32[1,8,64]{2,1,0:T(8,128)S(1)}, ...), condition=%wide.region_10.11_spmd.clone, body=%wide.region_7.10_spmd.clone.sunk | while | flops 136742464 | bytes 4234861 | solution.py:70
  489.7 1.3 fusion.76
  492.9 1.3 fusion.76
  496.0 1.3 fusion.76
  502.2 1.3 fusion.76
  505.4 1.3 fusion.76
  511.6 1.3 fusion.76
  513.6 15.0 %all_to_all.19 = bf16[8,8,1024]{2,1,0:T(8,128)(2,1)S(1)} all-to-all(bf16[8,8,1024]{2,1,0:T(8,128)(2,1)S(1)} %all_to_all.14), channel_id=1, replica_groups=mesh['ctx'=64,'head'=8] {'head'}, dimensions={0} | all-to-all | bytes 262144 | tf_op jit(solution)/shard_map/all_to_all | solution.py:106
  (442 shorter events, 131.1 us)
Async XLA Ops:
  6.5 150.6 %all-gather.5.cloned.1.call-start = ((), (), s32[]{:S(2)}) async-start(), calls=%async_computation.1 | async-start | bytes 5324800 | tf_op jit(solution)/shard_map/all_gather | solution.py:86
  7.3 286.6 %all-gather.7.cloned.1.call-start = ((), (), s32[]{:S(2)}) async-start(), calls=%async_computation.2 | async-start | bytes 5324800 | tf_op jit(solution)/shard_map/all_gather | solution.py:87
  8.0 410.4 %all-gather.9.cloned.1.call-start = ((), (), s32[]{:S(2)}) async-start(), calls=%async_computation.3 | async-start | bytes 1064960 | tf_op jit(solution)/shard_map/all_gather | solution.py:97
  8.7 479.6 %all-gather.11.cloned.1.call-start = ((), (), s32[]{:S(2)}) async-start(), calls=%async_computation.4 | async-start | bytes 1064960 | tf_op jit(solution)/shard_map/all_gather | solution.py:98
Sparse Core Ops, SparseCore 0:
  11.8 145.2 all-gather.4
  161.5 132.3 all-gather.6
  298.3 93.2 all-gather.8
  395.9 92.3 all-gather.10
where the time goes:
time: 539 us; the launch traced here: 536 us
  waiting for transfers between devices  352 us (65%)
  matrix products  123 us (23%)
  other arithmetic  26.8 us (5%)
  blocking collectives  15 us (3%)
  between operations  13.9 us (3%)
    all_gather x1, waiting for transfers between devices, per_device(): key_rows = lax.all_gather(prefix_key_slots, 'ctx', axis=0, tiled=True)  142 us
    all_gather x1, waiting for transfers between devices, per_device(): value_rows = lax.all_gather(prefix_value_slots, 'ctx', axis=0, tiled=True)  137 us
    all_gather x1, waiting for transfers between devices, per_device(): value_rows = lax.all_gather(suffix_value_rows, 'ctx', axis=0, tiled=True)  70 us
    dot_general x48, matrix products, update(): jnp.einsum('skgd,pkd->kgsp', query_heads, kb, preferred_element_type=jnp....  61.8 us
    dot_general x48, matrix products, update(): jnp.einsum('kgsp,pkd->kgsd', p.astype(jnp.bfloat16), vb, preferred_elemen...  61 us
    reduce_sum x48, other arithmetic, update(): total = total * factor + jnp.sum(p, axis=-1)  17.3 us
    all_to_all x1, blocking collectives, per_device(): lax.all_to_all(output, 'head', split_axis=0, concat_axis=1, tiled=True)  15 us
  transfers between devices with their start and end apart: 4, of which 3 were waited for; matrix products, arithmetic and copies ran while one was open for 24% of the time, Pallas kernels for 0%

commit v1 on v0

v1 whole, which is shorter than its diff:
```python
import math

import jax
import jax.numpy as jnp
from jax import lax
from jax.experimental import pallas as pl
from jax.experimental.pallas import tpu as pltpu
from jax.sharding import PartitionSpec as P

HEAD = 128
GROUP = 8
SUF = 64
POOL = 320
KEYS = POOL + SUF
WIDE = 2 * KEYS
VROWS = 144
COLS = SUF * GROUP
MSG = 80
SIDE = 4
HEADS = 8
NEG = -1e30
FACTOR = math.log2(math.e) / math.sqrt(HEAD)
MESH = pl.DeviceIdType.MESH


def kernel(
    q_ref, k_ref, vt_ref, span_ref, out_ref,
    kbuf, vbuf, qraw, qbuf, sbuf, acc, top, send, land, weights,
    s_first, r_first, s_line, r_line, s_core, r_core, s_q, r_q, s_out, r_out, s_own,
):
    ctx, zl = lax.axis_index("ctx"), lax.axis_index("head")
    c = ctx % 2
    x = ctx // 2 % SIDE
    y = ctx // (2 * SIDE) % SIDE
    zh = ctx // (2 * SIDE * SIDE)
    u = y * (1 - c) + x * c
    w = x * (1 - c) + y * c

    def place(plane, first, second, core):
        row = first * (1 - core) + second * core
        col = second * (1 - core) + first * core
        return ((plane * SIDE + row) * SIDE + col) * 2 + core

    def first(step):
        return (place(zh, (u + step) % SIDE, w, c), zl)

    def second(step):
        return (place(zh, u, (w + step) % SIDE, c), zl)

    partner = (ctx + 1 - 2 * c, zl)
    across = (place(1 - zh, u, w, c), zl)

    def column(flip, step):
        plane = (zh + flip) % 2
        return (place(plane, u, w, c), (zl + step) % HEADS)

    far = [(flip, step) for flip in (1, 0) for step in (4, 3, 5, 2, 6, 1, 7, 0) if flip or step]

    barrier = pltpu.get_barrier_semaphore()
    greeted = [column(f, s) for f, s in far]
    greeted += [first(1), first(2), first(3), second(1), second(3), partner]
    for who in greeted:
        pl.semaphore_signal(barrier, inc=1, device_id=who, device_id_type=MESH)

    def remote(src, dst, s_sem, r_sem, who):
        return pltpu.make_async_remote_copy(
            src_ref=src, dst_ref=dst, send_sem=s_sem, recv_sem=r_sem,
            device_id=who, device_id_type=MESH,
        )

    own_k = pltpu.make_async_copy(k_ref, kbuf.at[0, 0, pl.ds(0, KEYS)], s_own.at[0])
    own_v = pltpu.make_async_copy(vt_ref, vbuf.at[0, 0, :, pl.ds(0, KEYS)], s_own.at[1])
    own_k.start()
    own_v.start()

    def arrange(block):
        block = block.astype(jnp.float32)
        rows = [
            block[8 * z : 8 * z + 8, HEAD * g : HEAD * (g + 1)]
            for z in range(HEADS)
            for g in range(GROUP)
        ]
        return jnp.concatenate(rows, axis=0).astype(jnp.bfloat16)

    qbuf[0] = arrange(q_ref[...])
    acc[...] = jnp.zeros_like(acc)
    top[...] = jnp.full(top.shape, NEG, jnp.float32)

    pl.semaphore_wait(barrier, len(greeted))

    q_copy = remote(q_ref, qraw, s_q, r_q, across)
    q_copy.start()
    firsts = []
    for step in (1, 3, 2):
        chunk, half = step // 2, step % 2
        firsts.append(
            remote(k_ref, kbuf.at[0, chunk, pl.ds(half * KEYS, KEYS)],
                   s_first.at[step - 1], r_first.at[step - 1], first(step))
        )
        firsts.append(
            remote(vt_ref, vbuf.at[0, chunk, :, pl.ds(half * KEYS, KEYS)],
                   s_first.at[step + 2], r_first.at[step + 2], first(step))
        )
    for copy in firsts:
        copy.start()

    def scores(slot, chunk, part, queries):
        sbuf[part] = lax.dot_general(
            kbuf[slot, chunk], qbuf[queries], (((1,), (1,)), ((), ())),
            preferred_element_type=jnp.float32,
        )

    lead = lax.broadcasted_iota(jnp.int32, (SUF, COLS), 0)
    lane = lax.broadcasted_iota(jnp.int32, (SUF, COLS), 1)
    lead = lead - (lane // SUF * 8 + lane % 8)
    my_span = [span_ref[ctx], span_ref[place(1 - zh, u, w, c)]]

    def limit(slot, chunk, half, queries):
        whose = slot % 2
        batch = slot // 2
        core = c + whose - 2 * c * whose
        uu = u * (1 - whose) + w * whose
        ww = w * (1 - whose) + u * whose
        relative = chunk * 2 + half
        source = place(zh, (uu - relative + SIDE) % SIDE, (ww - batch + SIDE) % SIDE, core)
        return SUF * (my_span[queries] - span_ref[source])

    def absorb(slot, chunk, part, queries):
        pieces = []
        for half in range(2):
            base = half * KEYS
            pieces.append(sbuf[part, base : base + POOL])
            seen = lead <= limit(slot, chunk, half, queries)
            pieces.append(jnp.where(seen, sbuf[part, base + POOL : base + KEYS], NEG))
        peak = pieces[0].max(axis=0, keepdims=True)
        for piece in pieces[1:]:
            peak = jnp.maximum(peak, piece.max(axis=0, keepdims=True))
        old = top[queries, 0:1]
        new = jnp.maximum(old, peak * FACTOR)
        top[queries, 0:1] = new
        p = jnp.concatenate(
            [jnp.exp2(piece * FACTOR - new).astype(jnp.bfloat16) for piece in pieces], axis=0
        )
        acc[queries] = acc[queries] * jnp.exp2(old - new) + jnp.dot(
            vbuf[slot, chunk], p, preferred_element_type=jnp.float32
        )

    def line(slot, queries):
        scores(slot, 0, 0, queries)
        scores(slot, 1, 1, queries)
        absorb(slot, 0, 0, queries)
        absorb(slot, 1, 1, queries)

    def share(b, chunk):
        n = 2 * b + chunk
        return [
            remote(kbuf.at[2 * b, chunk], kbuf.at[2 * b + 1, chunk], s_core.at[n], r_core.at[n], partner),
            remote(vbuf.at[2 * b, chunk], vbuf.at[2 * b + 1, chunk], s_core.at[8 + n], r_core.at[8 + n], partner),
        ]

    def pass_on(source, target, chunk, n, who):
        return [
            remote(kbuf.at[2 * source, chunk], kbuf.at[2 * target, chunk], s_line.at[n], r_line.at[n], who),
            remote(vbuf.at[2 * source, chunk], vbuf.at[2 * target, chunk], s_line.at[6 + n], r_line.at[6 + n], who),
        ]

    def begin(copies):
        for copy in copies:
            copy.start()

    def arrived(copies):
        for copy in copies:
            copy.wait_recv()

    own_k.wait()
    own_v.wait()
    arrived(firsts)
    right = pass_on(0, 1, 0, 0, second(1)) + pass_on(0, 1, 1, 1, second(1))
    left = pass_on(0, 3, 0, 2, second(3)) + pass_on(0, 3, 1, 3, second(3))
    core = [share(b, chunk) for b in range(4) for chunk in range(2)]
    begin(right[:2] + left[2:] + right[2:] + left[:2])
    begin(core[0] + core[1])
    line(0, 0)
    arrived(core[0] + core[1])
    line(1, 0)
    turn_right = pass_on(1, 2, 0, 4, second(1))
    turn_left = pass_on(3, 2, 1, 5, second(3))
    arrived(right[:2])
    begin(turn_right)
    arrived(left[2:])
    begin(turn_left)
    arrived(right[2:])
    begin(core[2] + core[3])
    arrived(left[:2])
    begin(core[6] + core[7])
    line(2, 0)
    line(6, 0)
    arrived(core[2] + core[3])
    line(3, 0)
    arrived(turn_right + turn_left)
    begin(core[4] + core[5])
    arrived(core[6] + core[7])
    line(7, 0)
    line(4, 0)
    arrived(core[4] + core[5])
    line(5, 0)

    def finish(queries):
        total = acc[queries, HEAD : HEAD + 1]
        values = (acc[queries, 0:HEAD] * (1.0 / total)).T
        level = top[queries, 0:1] + jnp.log2(total)
        high = level.astype(jnp.bfloat16).astype(jnp.float32)
        middle = (level - high).astype(jnp.bfloat16).astype(jnp.float32)
        low = level - high - middle
        row = lax.broadcasted_iota(jnp.int32, (16, COLS), 0)
        stats = jnp.where(row == 0, high, jnp.where(row == 1, middle, jnp.where(row == 2, low, 0.0)))
        for z in range(HEADS):
            send[queries, z, 0:SUF] = values[SUF * z : SUF * (z + 1)].astype(jnp.bfloat16)
            near = z // 2 * HEAD
            send[queries, z, SUF:MSG] = stats[:, near : near + HEAD].astype(jnp.bfloat16)

    outs = {}
    for n, (flip, step) in enumerate(far):
        outs[flip, step] = remote(
            send.at[flip, (zl + step) % HEADS], land.at[flip, zl], s_out.at[n], r_out.at[n], column(flip, step)
        )
    finish(0)
    for step in (4, 3, 5, 2, 6, 1, 7):
        outs[0, step].start()
    land[0, zl] = send[0, zl]

    q_copy.wait_recv()
    qbuf[1] = arrange(qraw[...])

    def step_over(slot, carry):
        line(slot, 1)
        return carry

    lax.fori_loop(0, 8, step_over, 0)
    finish(1)
    for step in (4, 3, 5, 2, 6, 1, 7, 0):
        outs[1, step].start()

    for copy in outs.values():
        copy.wait_recv()

    def level_of(flip):
        rows = []
        for z in range(HEADS):
            tile = land[flip, z, SUF:MSG].astype(jnp.float32)
            rows.append(tile[0:1] + tile[1:2] + tile[2:3])
        return jnp.concatenate(rows, axis=0)

    near, other = level_of(0), level_of(1)
    peak = jnp.maximum(near, other)
    near, other = jnp.exp2(near - peak), jnp.exp2(other - peak)
    both = near + other
    weights[...] = jnp.concatenate([near / both, other / both], axis=0).T
    shares = weights[pl.ds(pl.multiple_of(zl % 2 * SUF, SUF), SUF)]
    for z in range(HEADS):
        o = land[0, z, 0:SUF].astype(jnp.float32) * shares[:, z : z + 1]
        o = o + land[1, z, 0:SUF].astype(jnp.float32) * shares[:, HEADS + z : HEADS + z + 1]
        row = jnp.concatenate([o[8 * g : 8 * g + 8] for g in range(GROUP)], axis=1)
        out_ref[:, z * GROUP * HEAD : (z + 1) * GROUP * HEAD] = row.astype(jnp.bfloat16)

    for copy in [q_copy] + firsts + right + left + turn_right + turn_left:
        copy.wait_send()
    for pair in core:
        for copy in pair:
            copy.wait_send()
    for copy in outs.values():
        copy.wait_send()


def per_device(queries, suffix_keys, suffix_values, prefix_keys, prefix_values, counts, span_order):
    ctx = lax.axis_index("ctx")
    count = lax.dynamic_slice(counts, (ctx,), (1,))[0]
    live = (jnp.arange(POOL) < count)[:, None]
    keys = jnp.concatenate([jnp.where(live, prefix_keys, prefix_keys[0:1]), suffix_keys])
    values = jnp.concatenate([jnp.where(live, prefix_values, 0), suffix_values])
    place = jnp.arange(KEYS)[None, :]
    ones = ((place < count) | (place >= POOL)) & (jnp.arange(VROWS - HEAD)[:, None] == 0)
    values = jnp.concatenate([values.T, ones.astype(jnp.bfloat16)])
    vmem = pl.BlockSpec(memory_space=pltpu.VMEM)
    dma = pltpu.SemaphoreType.DMA
    bf16, f32 = jnp.bfloat16, jnp.float32
    return pl.pallas_call(
        kernel,
        out_shape=jax.ShapeDtypeStruct((SUF // HEADS, HEADS * GROUP * HEAD), bf16),
        in_specs=[vmem, vmem, vmem, pl.BlockSpec(memory_space=pltpu.SMEM)],
        out_specs=vmem,
        scratch_shapes=[
            pltpu.VMEM((8, 2, WIDE, HEAD), bf16),
            pltpu.VMEM((8, 2, VROWS, WIDE), bf16),
            pltpu.VMEM((SUF, GROUP * HEAD), bf16),
            pltpu.VMEM((2, COLS, HEAD), bf16),
            pltpu.VMEM((2, WIDE, COLS), f32),
            pltpu.VMEM((2, VROWS, COLS), f32),
            pltpu.VMEM((2, 8, COLS), f32),
            pltpu.VMEM((2, HEADS, MSG, HEAD), bf16),
            pltpu.VMEM((2, HEADS, MSG, HEAD), bf16),
            pltpu.VMEM((HEAD, 2 * HEADS), f32),
            dma((6,)), dma((6,)), dma((12,)), dma((12,)), dma((16,)), dma((16,)),
            dma, dma, dma((15,)), dma((15,)), dma((2,)),
        ],
        compiler_params=pltpu.CompilerParams(
            collective_id=0, has_side_effects=True, vmem_limit_bytes=48 << 20
        ),
    )(queries, keys, values, span_order)


def solution(mesh):
    two = P("ctx", "head")
    return jax.shard_map(
        per_device,
        mesh=mesh,
        in_specs=(two, two, two, two, two, P(), P()),
        out_specs=P(("ctx", "head"), None),
        check_vma=False,
    )
```

time: 539 us -> 81.4 us (0.15)
  the two profiles are of different devices: /device:TPU:6 before, /device:TPU:33 now
where the time goes in v1:
time: 81.4 us; the launch traced here: 81.1 us
  Pallas kernels  74 us (91%)
  local copies, waits for them, and re-layouts  5.39 us (7%)
  other arithmetic  1.59 us (2%)
    pallas_call x1, Pallas kernels, per_device(): pl.pallas_call(kernel, out_shape=jax.ShapeDtypeStruct((SUF // HEADS, HEAD...  74 us
    unnamed x17, local copies, waits for them, and re-layouts  4.69 us

profile of v1, /device:TPU:33, one launch (start us, length us, event | category | flops | bytes accessed | tf_op | source)
XLA Modules:
  0.0 81.1 jit_solution(5836241617025050551)
XLA Ops:
  0.0 0.0 copy-start.5
  0.0 0.7 copy-done.5
  0.7 0.6 dynamic_slice.3
  1.2 0.6 iota_compare_fusion.2
  1.9 0.0 copy-start.2
  1.9 1.0 %copy.10 = bf16[320,128]{0,1:T(8,128)(2,1)S(1)} copy(bf16[320,128]{1,0:T(8,128)(2,1)} %param.11) | data formatting | bytes 163840 | tf_op args[4]
  2.9 0.0 copy-done.2
  3.0 0.1 copy.8
  3.1 0.0 copy-start.3
  3.1 0.1 broadcast_select_fusion
  3.2 0.6 copy-done.3
  3.8 0.1 copy.11
  3.9 0.6 copy-done.4
  4.5 0.1 copy.9
  4.6 0.1 pad_maximum_fusion.1
  4.8 0.7 fusion
  5.4 0.1 and_convert_fusion
  5.5 0.0 copy-start
  5.5 0.0 copy-start.1
  5.5 0.1 copy.12.k_ref
  5.7 0.8 copy-done
  6.4 0.0 copy-done.1
  6.4 74.0 %shard_map.73 = bf16[8,8192]{1,0:T(8,128)(2,1)S(1)} custom-call(bf16[64,1024]{1,0:T(8,128)(2,1)S(1)} %copy-done, bf16[384,128]{1,0:T(8,128)(2,1)S(1)} %copy.12.k_ref, bf16[144,384]{1,0:T(8,128)(2,1)S(1)} %pad_maximum_fusion.vt_ref, s32[64]{0:T(128)S(1)} %copy-done.1), custom_call_target="tpu_custom_call" | custom-call | tf_op jit(solution)/shard_map/pallas_call | solution.py:287
  80.4 0.7 copy.14
  (4 shorter events, 0.0 us)
Async XLA Ops:
  0.0 0.7 copy-start.5
  1.9 1.1 %copy-start.2 = (bf16[320,128]{1,0:T(8,128)(2,1)S(1)}, bf16[320,128]{1,0:T(8,128)(2,1)}, u32[]{:S(2)}) copy-start(bf16[320,128]{1,0:T(8,128)(2,1)} %param.10) | copy-start | bytes 245764
  3.1 0.7 copy-start.3
  3.8 0.7 copy-start.4
  5.5 0.9 %copy-start = (bf16[64,1024]{1,0:T(8,128)(2,1)S(1)}, bf16[64,1024]{1,0:T(8,128)(2,1)}, u32[]{:S(2)}) copy-start(bf16[64,1024]{1,0:T(8,128)(2,1)} %q_ref.1) | copy-start | bytes 393220
  5.5 0.9 %copy-start.1 = (s32[64]{0:T(128)S(1)}, s32[64]{0:T(128)}, u32[]{:S(2)}) copy-start(s32[64]{0:T(128)} %span_ref.1) | copy-start | bytes 772

commit v2 on v1

v2 whole, which is shorter than its diff:
```python
import math

import jax
import jax.numpy as jnp
from jax import lax
from jax.experimental import pallas as pl
from jax.experimental.pallas import tpu as pltpu
from jax.sharding import PartitionSpec as P

HEAD = 128
GROUP = 8
SUF = 64
POOL = 320
KEYS = POOL + SUF
WIDE = 2 * KEYS
VROWS = 144
COLS = SUF * GROUP
LIMIT = 63 << 20
SIDE = 4
HEADS = 8
NEG = -1e30
FACTOR = math.log2(math.e) / math.sqrt(HEAD)
MESH = pl.DeviceIdType.MESH


def kernel(
    q_ref, sk_ref, sv_ref, pk_ref, pv_ref, count_ref, span_ref, out_ref,
    kbuf, vbuf, qown, skv, pkv, qraw, qbuf, sbuf, acc, top, send, land, level_send, level_land, weights,
    s_first, r_first, s_line, r_line, s_core, r_core, s_q, r_q, s_out, r_out, s_own, reach,
):
    ctx, zl = lax.axis_index("ctx"), lax.axis_index("head")
    c = ctx % 2
    x = ctx // 2 % SIDE
    y = ctx // (2 * SIDE) % SIDE
    zh = ctx // (2 * SIDE * SIDE)
    u = y * (1 - c) + x * c
    w = x * (1 - c) + y * c

    def place(plane, first, second, core):
        row = first * (1 - core) + second * core
        col = second * (1 - core) + first * core
        return ((plane * SIDE + row) * SIDE + col) * 2 + core

    def first(step):
        return (place(zh, (u + step) % SIDE, w, c), zl)

    def second(step):
        return (place(zh, u, (w + step) % SIDE, c), zl)

    partner = (ctx + 1 - 2 * c, zl)
    across = (place(1 - zh, u, w, c), zl)

    def column(flip, step):
        plane = (zh + flip) % 2
        return (place(plane, u, w, c), (zl + step) % HEADS)

    far = [(flip, step) for flip in (1, 0) for step in (4, 3, 5, 2, 6, 1, 7, 0) if flip or step]

    barrier = pltpu.get_barrier_semaphore()

    def along(step):
        z = (zh * HEADS + zl + step) % (2 * HEADS)
        return (place(z // HEADS, u, w, c), z % HEADS)

    greeted = [first(1), first(2), first(3), second(1), second(3), partner, along(1), along(15)]
    for who in greeted:
        pl.semaphore_signal(barrier, inc=1, device_id=who, device_id_type=MESH)

    def remote(src, dst, s_sem, r_sem, who):
        return pltpu.make_async_remote_copy(
            src_ref=src, dst_ref=dst, send_sem=s_sem, recv_sem=r_sem,
            device_id=who, device_id_type=MESH,
        )

    loads = [
        pltpu.make_async_copy(source, target, s_own.at[n])
        for n, (source, target) in enumerate(
            [(pk_ref, pkv.at[0]), (sk_ref, skv.at[0]), (pv_ref, pkv.at[1]), (sv_ref, skv.at[1]), (q_ref, qown)]
        )
    ]
    for load in loads:
        load.start()

    def arrange(block):
        block = block.astype(jnp.float32)
        rows = [
            block[8 * z : 8 * z + 8, HEAD * g : HEAD * (g + 1)]
            for z in range(HEADS)
            for g in range(GROUP)
        ]
        return jnp.concatenate(rows, axis=0).astype(jnp.bfloat16)

    acc[...] = jnp.zeros_like(acc)
    top[...] = jnp.full(top.shape, NEG, jnp.float32)

    def batch_of(slot):
        rank = slot // 2
        return rank + rank // 2 - rank // 3 * 2

    def source_of(slot, chunk, half):
        whose = slot % 2
        core = c + whose - 2 * c * whose
        uu = u * (1 - whose) + w * whose
        ww = w * (1 - whose) + u * whose
        relative = chunk * 2 + half
        return place(zh, (uu - relative + SIDE) % SIDE, (ww - batch_of(slot) + SIDE) % SIDE, core)

    one_row = lax.broadcasted_iota(jnp.int32, (VROWS - HEAD, KEYS), 0)
    one_col = lax.broadcasted_iota(jnp.int32, (VROWS - HEAD, KEYS), 1)

    def ones_of(slot, carry):
        for chunk in range(2):
            for half in range(2):
                count = count_ref[source_of(slot, chunk, half)]
                row = jnp.where((one_row == 0) & ((one_col < count) | (one_col >= POOL)), 1.0, 0.0)
                vbuf[slot, chunk, HEAD:VROWS, half * KEYS : (half + 1) * KEYS] = row.astype(jnp.bfloat16)
        return carry

    lax.fori_loop(0, 8, ones_of, 0)

    for load in loads:
        load.wait()
    live = lax.broadcasted_iota(jnp.int32, (POOL, HEAD), 0) < count_ref[ctx]
    rows = pkv[0].astype(jnp.float32)
    kbuf[0, 0, 0:POOL] = jnp.where(live, rows, rows[0:1]).astype(jnp.bfloat16)
    kbuf[0, 0, POOL:KEYS] = skv[0]
    rows = jnp.where(live, pkv[1].astype(jnp.float32), 0.0)
    rows = jnp.concatenate([rows, skv[1].astype(jnp.float32)], axis=0)
    vbuf[0, 0, 0:HEAD, 0:KEYS] = rows.T.astype(jnp.bfloat16)

    pl.semaphore_wait(barrier, len(greeted))

    def keys_at(slot, piece):
        return kbuf.at[slot, piece // 2, pl.ds(piece % 2 * KEYS, KEYS)]

    def values_at(slot, piece):
        return vbuf.at[slot, piece // 2, pl.ds(0, HEAD), pl.ds(piece % 2 * KEYS, KEYS)]

    def forward(source, target, piece, n, s_sem, r_sem, who):
        begins = 0 if s_sem is s_first else piece
        return [
            remote(keys_at(source, begins), keys_at(target, piece), s_sem.at[2 * n], r_sem.at[2 * n], who),
            remote(values_at(source, begins), values_at(target, piece), s_sem.at[2 * n + 1], r_sem.at[2 * n + 1], who),
        ]

    def begin(*groups):
        for group in groups:
            for copy in group:
                copy.start()

    def arrived(*groups):
        for group in groups:
            for copy in group:
                copy.wait_recv()

    ahead = {r: forward(0, 0, r, r - 1, s_first, r_first, first(r)) for r in (1, 3, 2)}
    right = [forward(0, 2, r, r, s_line, r_line, second(1)) for r in range(4)]
    left = [forward(0, 4, r, 4 + r, s_line, r_line, second(3)) for r in range(4)]
    turn_right = [forward(2, 6, r, 8 + r, s_line, r_line, second(1)) for r in (0, 1)]
    turn_left = [forward(4, 6, r, 8 + r, s_line, r_line, second(3)) for r in (2, 3)]
    q_copy = remote(qown, qraw, s_q, r_q, across)
    begin(ahead[1], ahead[3], right[0], left[0], ahead[2])
    for n in range(3):
        for step in (1 << n, 16 - (1 << n)):
            pl.semaphore_signal(reach.at[n], inc=1, device_id=along(step), device_id_type=MESH)
        pl.semaphore_wait(reach.at[n], 2)
    q_copy.start()
    qbuf[0] = arrange(qown[...])

    def scores(slot, chunk, part, queries):
        sbuf[part] = lax.dot_general(
            kbuf[slot, chunk], qbuf[queries], (((1,), (1,)), ((), ())),
            preferred_element_type=jnp.float32,
        )

    lead = lax.broadcasted_iota(jnp.int32, (SUF, COLS), 0)
    lane = lax.broadcasted_iota(jnp.int32, (SUF, COLS), 1)
    lead = lead - (lane // SUF * 8 + lane % 8)
    my_span = [span_ref[ctx], span_ref[place(1 - zh, u, w, c)]]

    def limit(slot, chunk, half, queries):
        return SUF * (my_span[queries] - span_ref[source_of(slot, chunk, half)])

    def absorb(slot, chunk, part, queries):
        pieces = []
        for half in range(2):
            base = half * KEYS
            pieces.append(sbuf[part, base : base + POOL])
            seen = lead <= limit(slot, chunk, half, queries)
            pieces.append(jnp.where(seen, sbuf[part, base + POOL : base + KEYS], NEG))
        peak = pieces[0].max(axis=0, keepdims=True)
        for piece in pieces[1:]:
            peak = jnp.maximum(peak, piece.max(axis=0, keepdims=True))
        old = top[queries, 0:1]
        new = jnp.maximum(old, peak * FACTOR)
        top[queries, 0:1] = new
        p = jnp.concatenate(
            [jnp.exp2(piece * FACTOR - new).astype(jnp.bfloat16) for piece in pieces], axis=0
        )
        acc[queries] = acc[queries] * jnp.exp2(old - new) + jnp.dot(
            vbuf[slot, chunk], p, preferred_element_type=jnp.float32
        )

    def sweep(count, pick, queries):
        scores(*pick(0, 0), 0, queries)

        def pair(i, carry):
            later = jnp.minimum(i + 1, count - 1)
            scores(*pick(i, 1), 1, queries)
            absorb(*pick(i, 0), 0, queries)
            scores(*pick(later, 0), 0, queries)
            absorb(*pick(i, 1), 1, queries)
            return carry

        lax.fori_loop(0, count, pair, 0)

    def share(r, chunk):
        n = 2 * r + chunk
        rows = pl.ds(0, HEAD)
        return [
            remote(kbuf.at[2 * r, chunk], kbuf.at[2 * r + 1, chunk], s_core.at[n], r_core.at[n], partner),
            remote(vbuf.at[2 * r, chunk, rows], vbuf.at[2 * r + 1, chunk, rows], s_core.at[8 + n], r_core.at[8 + n], partner),
        ]

    core = [[share(r, chunk) for chunk in range(2)] for r in range(4)]
    arrived(ahead[1])
    begin(right[1], left[1], core[0][0])
    arrived(right[0])
    begin(turn_right[0])
    arrived(ahead[3])
    begin(right[3], left[3])
    arrived(ahead[2])
    begin(right[2], left[2], core[0][1])
    sweep(1, lambda i, j: (0, j), 0)
    arrived(*core[0])
    sweep(1, lambda i, j: (1, j), 0)
    arrived(right[1])
    begin(turn_right[1], core[1][0])
    arrived(left[3])
    begin(turn_left[1])
    arrived(left[0], left[1])
    begin(core[2][0])
    sweep(1, lambda i, j: (2 + 2 * j, 0), 0)
    arrived(right[3], right[2])
    begin(core[1][1])
    arrived(left[2])
    begin(turn_left[0], core[2][1])
    arrived(core[1][0], core[2][0])
    sweep(1, lambda i, j: (3 + 2 * j, 0), 0)
    sweep(1, lambda i, j: (2 + 2 * j, 1), 0)
    arrived(core[1][1], core[2][1])
    sweep(1, lambda i, j: (3 + 2 * j, 1), 0)
    q_copy.wait_recv()
    qbuf[1] = arrange(qraw[...])
    sweep(3, lambda i, j: (i, j), 1)
    arrived(*turn_right)
    begin(core[3][0])
    arrived(*turn_left)
    begin(core[3][1])
    sweep(3, lambda i, j: (3 + i, j), 1)
    arrived(*core[3])
    sweep(2, lambda i, j: (6 + i, j), 1)

    def finish(queries):
        total = acc[queries, HEAD : HEAD + 1]
        values = (acc[queries, 0:HEAD] * (1.0 / total)).T
        level = top[queries, 0:1] + jnp.log2(total)
        for z in range(HEADS):
            send[queries, z] = values[SUF * z : SUF * (z + 1)].astype(jnp.bfloat16)
            near = z // 2 * HEAD
            level_send[queries, z, 0:1] = level[:, near : near + HEAD]

    outs = {}
    for n, (flip, step) in enumerate(far):
        who, to = column(flip, step), (zl + step) % HEADS
        row = pl.ds(0, 1)
        outs[flip, step] = [
            remote(level_send.at[flip, to, row], level_land.at[flip, zl, row], s_out.at[n], r_out.at[n], who),
            remote(send.at[flip, to], land.at[flip, zl], s_out.at[15 + n], r_out.at[15 + n], who),
        ]
    finish(1)
    for step in (4, 3, 5, 2, 6, 1, 7, 0):
        begin(outs[1, step])
    sweep(2, lambda i, j: (6 + i, j), 0)
    finish(0)
    for step in (4, 3, 5, 2, 6, 1, 7):
        begin(outs[0, step])
    land[0, zl] = send[0, zl]
    level_land[0, zl, 0:1] = level_send[0, zl, 0:1]

    arrived(*outs.values())

    def level_of(flip):
        return jnp.concatenate([level_land[flip, z, 0:1] for z in range(HEADS)], axis=0)

    near, other = level_of(0), level_of(1)
    peak = jnp.maximum(near, other)
    near, other = jnp.exp2(near - peak), jnp.exp2(other - peak)
    both = near + other
    weights[...] = jnp.concatenate([near / both, other / both], axis=0).T
    shares = weights[pl.ds(pl.multiple_of(zl % 2 * SUF, SUF), SUF)]
    for z in range(HEADS):
        o = land[0, z].astype(jnp.float32) * shares[:, z : z + 1]
        o = o + land[1, z].astype(jnp.float32) * shares[:, HEADS + z : HEADS + z + 1]
        row = jnp.concatenate([o[8 * g : 8 * g + 8] for g in range(GROUP)], axis=1)
        out_ref[:, z * GROUP * HEAD : (z + 1) * GROUP * HEAD] = row.astype(jnp.bfloat16)

    q_copy.wait_send()
    for group in [*ahead.values(), *right, *left, *turn_right, *turn_left, *core[0], *core[1], *core[2], *core[3], *outs.values()]:
        for copy in group:
            copy.wait_send()


def per_device(queries, suffix_keys, suffix_values, prefix_keys, prefix_values, counts, span_order):
    smem = pl.BlockSpec(memory_space=pltpu.SMEM)
    stays = pl.BlockSpec(memory_space=pltpu.HBM)
    vmem = pl.BlockSpec(memory_space=pltpu.VMEM)
    dma = pltpu.SemaphoreType.DMA
    bf16, f32 = jnp.bfloat16, jnp.float32
    return pl.pallas_call(
        kernel,
        out_shape=jax.ShapeDtypeStruct((SUF // HEADS, HEADS * GROUP * HEAD), bf16),
        in_specs=[stays] * 5 + [smem] * 2,
        out_specs=vmem,
        scratch_shapes=[
            pltpu.VMEM((8, 2, WIDE, HEAD), bf16),
            pltpu.VMEM((8, 2, VROWS, WIDE), bf16),
            pltpu.VMEM((SUF, GROUP * HEAD), bf16),
            pltpu.VMEM((2, SUF, HEAD), bf16),
            pltpu.VMEM((2, POOL, HEAD), bf16),
            pltpu.VMEM((SUF, GROUP * HEAD), bf16),
            pltpu.VMEM((2, COLS, HEAD), bf16),
            pltpu.VMEM((2, WIDE, COLS), f32),
            pltpu.VMEM((2, VROWS, COLS), f32),
            pltpu.VMEM((2, 8, COLS), f32),
            pltpu.VMEM((2, HEADS, SUF, HEAD), bf16),
            pltpu.VMEM((2, HEADS, SUF, HEAD), bf16),
            pltpu.VMEM((2, HEADS, 8, HEAD), f32),
            pltpu.VMEM((2, HEADS, 8, HEAD), f32),
            pltpu.VMEM((HEAD, 2 * HEADS), f32),
            dma((6,)), dma((6,)), dma((24,)), dma((24,)), dma((16,)), dma((16,)),
            dma, dma, dma((30,)), dma((30,)), dma((5,)), pltpu.SemaphoreType.REGULAR((3,)),
        ],
        compiler_params=pltpu.CompilerParams(
            collective_id=0, has_side_effects=True, vmem_limit_bytes=LIMIT
        ),
    )(queries, suffix_keys, suffix_values, prefix_keys, prefix_values, counts, span_order)


def solution(mesh):
    two = P("ctx", "head")
    return jax.shard_map(
        per_device,
        mesh=mesh,
        in_specs=(two, two, two, two, two, P(), P()),
        out_specs=P(("ctx", "head"), None),
        check_vma=False,
    )
```

time: 81.4 us -> 65 us (0.80)
  the two profiles are of different devices: /device:TPU:33 before, /device:TPU:32 now
where the time goes in v2:
time: 65 us; the launch traced here: 64.8 us
  Pallas kernels  63.2 us (97%)
  local copies, waits for them, and re-layouts  1.57 us (2%)
    pallas_call x1, Pallas kernels, per_device(): pl.pallas_call(kernel, out_shape=jax.ShapeDtypeStruct((SUF // HEADS, HEAD...  63.2 us
    unnamed x1, local copies, waits for them, and re-layouts  1.57 us

profile of v2, /device:TPU:32, one launch (start us, length us, event | category | flops | bytes accessed | tf_op | source)
XLA Modules:
  0.0 64.8 jit_solution(11912804810386901771)
XLA Ops:
  0.0 63.2 %shard_map.73 = bf16[8,8192]{1,0:T(8,128)(2,1)} custom-call(bf16[64,1024]{1,0:T(8,128)(2,1)} %q_ref.1, bf16[64,128]{1,0:T(8,128)(2,1)} %sk_ref.1, bf16[64,128]{1,0:T(8,128)(2,1)} %sv_ref.1, bf16[320,128]{1,0:T(8,128)(2,1)} %pk_ref.1, bf16[320,128]{1,0:T(8,128)(2,1)} %pv_ref.1, s32[64]{0:T(128)} %count_ref.1, s32[64]{0:T(128)} %span_ref.1), custom_call_target="tpu_custom_call" | custom-call | tf_op jit(solution)/shard_map/pallas_call | solution.py:320
  63.2 1.6 %copy.9 = bf16[8,8192]{1,0:T(8,128)(2,1)} copy(bf16[8,8192]{1,0:T(8,128)(2,1)} %shard_map.73) | data formatting | bytes 262144

commit v3 on v2

--- a/solution.py
+++ b/solution.py
@@ -25,7 +25,7 @@
 
 def kernel(
     q_ref, sk_ref, sv_ref, pk_ref, pv_ref, count_ref, span_ref, out_ref,
-    kbuf, vbuf, qown, skv, pkv, qraw, qbuf, sbuf, acc, top, send, land, level_send, level_land, weights,
+    kbuf, vbuf, qown, skv, pkv, qraw, qbuf, sbuf, acc, top, send, land, level_send, level_land, flat, share_of, weights,
     s_first, r_first, s_line, r_line, s_core, r_core, s_q, r_q, s_out, r_out, s_own, reach,
 ):
     ctx, zl = lax.axis_index("ctx"), lax.axis_index("head")
@@ -62,7 +62,8 @@
         z = (zh * HEADS + zl + step) % (2 * HEADS)
         return (place(z // HEADS, u, w, c), z % HEADS)
 
-    greeted = [first(1), first(2), first(3), second(1), second(3), partner, along(1), along(15)]
+    greeted = [first(1), first(2), first(3), second(1), second(3), partner]
+    greeted += [along(step) for k in (1, 2, 3, 4) for step in (k, 16 - k)]
     for who in greeted:
         pl.semaphore_signal(barrier, inc=1, device_id=who, device_id_type=MESH)
 
@@ -156,12 +157,14 @@
     ahead = {r: forward(0, 0, r, r - 1, s_first, r_first, first(r)) for r in (1, 3, 2)}
     right = [forward(0, 2, r, r, s_line, r_line, second(1)) for r in range(4)]
     left = [forward(0, 4, r, 4 + r, s_line, r_line, second(3)) for r in range(4)]
-    turn_right = [forward(2, 6, r, 8 + r, s_line, r_line, second(1)) for r in (0, 1)]
-    turn_left = [forward(4, 6, r, 8 + r, s_line, r_line, second(3)) for r in (2, 3)]
+    turn_right = forward(2, 6, 0, 8, s_line, r_line, second(1))
+    turn_left = forward(4, 6, 3, 11, s_line, r_line, second(3))
+    turn_keys = {r: [forward(2, 6, r, 8 + r, s_line, r_line, second(1))[0]] for r in (1, 2)}
+    turn_values = {r: [forward(4, 6, r, 8 + r, s_line, r_line, second(3))[1]] for r in (1, 2)}
     q_copy = remote(qown, qraw, s_q, r_q, across)
     begin(ahead[1], ahead[3], right[0], left[0], ahead[2])
-    for n in range(3):
-        for step in (1 << n, 16 - (1 << n)):
+    for n, k in enumerate((4,)):
+        for step in (k, 16 - k):
             pl.semaphore_signal(reach.at[n], inc=1, device_id=along(step), device_id_type=MESH)
         pl.semaphore_wait(reach.at[n], 2)
     q_copy.start()
@@ -223,52 +226,67 @@
         ]
 
     core = [[share(r, chunk) for chunk in range(2)] for r in range(4)]
-    arrived(ahead[1])
-    begin(right[1], left[1], core[0][0])
-    arrived(right[0])
-    begin(turn_right[0])
-    arrived(ahead[3])
-    begin(right[3], left[3])
-    arrived(ahead[2])
-    begin(right[2], left[2], core[0][1])
-    sweep(1, lambda i, j: (0, j), 0)
-    arrived(*core[0])
-    sweep(1, lambda i, j: (1, j), 0)
-    arrived(right[1])
-    begin(turn_right[1], core[1][0])
-    arrived(left[3])
-    begin(turn_left[1])
-    arrived(left[0], left[1])
+    def hop(source, *targets):
+        for n in range(2):
+            arrived(source[n : n + 1])
+            begin(*[target[n : n + 1] for target in targets])
+
+    hop(ahead[1], right[1], left[1])
+    begin(core[0][0])
+    hop(ahead[3], right[3], left[3])
+    hop(ahead[2], right[2], left[2])
+    begin(core[0][1])
+    hop(right[0], turn_right)
+    arrived(core[0][0])
+    sweep(1, lambda i, j: (j, 0), 0)
+    arrived(right[1][:1])
+    begin(turn_keys[1])
+    arrived(left[1][1:])
+    begin(turn_values[1])
+    hop(left[3], turn_left)
+    arrived(right[1][1:])
+    begin(core[1][0])
+    arrived(left[0], left[1][:1])
     begin(core[2][0])
+    arrived(core[0][1])
+    sweep(1, lambda i, j: (j, 1), 0)
     sweep(1, lambda i, j: (2 + 2 * j, 0), 0)
-    arrived(right[3], right[2])
+    arrived(right[2][:1])
+    begin(turn_keys[2])
+    arrived(left[2][1:])
+    begin(turn_values[2])
+    arrived(left[2][:1])
+    begin(core[2][1])
+    arrived(right[2][1:], right[3])
     begin(core[1][1])
-    arrived(left[2])
-    begin(turn_left[0], core[2][1])
     arrived(core[1][0], core[2][0])
     sweep(1, lambda i, j: (3 + 2 * j, 0), 0)
-    sweep(1, lambda i, j: (2 + 2 * j, 1), 0)
-    arrived(core[1][1], core[2][1])
-    sweep(1, lambda i, j: (3 + 2 * j, 1), 0)
     q_copy.wait_recv()
     qbuf[1] = arrange(qraw[...])
-    sweep(3, lambda i, j: (i, j), 1)
-    arrived(*turn_right)
+    sweep(2, lambda i, j: (i, j), 1)
+    arrived(turn_right, turn_keys[1], turn_values[1])
     begin(core[3][0])
-    arrived(*turn_left)
+    arrived(core[1][1], core[2][1])
+    sweep(2, lambda i, j: (2 + i, j), 1)
+    arrived(turn_left, turn_keys[2], turn_values[2])
     begin(core[3][1])
-    sweep(3, lambda i, j: (3 + i, j), 1)
+    sweep(3, lambda i, j: (4 + i, j), 1)
     arrived(*core[3])
-    sweep(2, lambda i, j: (6 + i, j), 1)
-
-    def finish(queries):
+    sweep(1, lambda i, j: (7, j), 1)
+
+    def finish(queries, order):
         total = acc[queries, HEAD : HEAD + 1]
-        values = (acc[queries, 0:HEAD] * (1.0 / total)).T
         level = top[queries, 0:1] + jnp.log2(total)
         for z in range(HEADS):
-            send[queries, z] = values[SUF * z : SUF * (z + 1)].astype(jnp.bfloat16)
             near = z // 2 * HEAD
             level_send[queries, z, 0:1] = level[:, near : near + HEAD]
+        for step in order:
+            begin(outs[queries, step][:1])
+        flat[...] = (acc[queries, 0:HEAD] * (1.0 / total)).T
+        for step in order:
+            to = (zl + step) % HEADS
+            send[queries, to] = flat[pl.ds(pl.multiple_of(to * SUF, SUF), SUF)].astype(jnp.bfloat16)
+            begin(outs[queries, step][1:])
 
     outs = {}
     for n, (flip, step) in enumerate(far):
@@ -278,17 +296,14 @@
             remote(level_send.at[flip, to, row], level_land.at[flip, zl, row], s_out.at[n], r_out.at[n], who),
             remote(send.at[flip, to], land.at[flip, zl], s_out.at[15 + n], r_out.at[15 + n], who),
         ]
-    finish(1)
-    for step in (4, 3, 5, 2, 6, 1, 7, 0):
-        begin(outs[1, step])
+    finish(1, (4, 3, 5, 2, 6, 1, 7, 0))
+    sweep(2, lambda i, j: (2 + 2 * i + j, 1), 0)
     sweep(2, lambda i, j: (6 + i, j), 0)
-    finish(0)
-    for step in (4, 3, 5, 2, 6, 1, 7):
-        begin(outs[0, step])
+    finish(0, (4, 3, 5, 2, 6, 1, 7))
+    send[0, zl] = flat[pl.ds(pl.multiple_of(zl * SUF, SUF), SUF)].astype(jnp.bfloat16)
     land[0, zl] = send[0, zl]
     level_land[0, zl, 0:1] = level_send[0, zl, 0:1]
-
-    arrived(*outs.values())
+    arrived(*[copies[:1] for copies in outs.values()])
 
     def level_of(flip):
         return jnp.concatenate([level_land[flip, z, 0:1] for z in range(HEADS)], axis=0)
@@ -299,14 +314,21 @@
     both = near + other
     weights[...] = jnp.concatenate([near / both, other / both], axis=0).T
     shares = weights[pl.ds(pl.multiple_of(zl % 2 * SUF, SUF), SUF)]
-    for z in range(HEADS):
-        o = land[0, z].astype(jnp.float32) * shares[:, z : z + 1]
-        o = o + land[1, z].astype(jnp.float32) * shares[:, HEADS + z : HEADS + z + 1]
+    for n in range(2 * HEADS):
+        share_of[n] = jnp.broadcast_to(shares[:, n : n + 1], (SUF, HEAD))
+    for step in (0, 4, 3, 5, 2, 6, 1, 7):
+        z = (zl + HEADS - step) % HEADS
+        arrived(outs[1, step][1:])
+        if step:
+            arrived(outs[0, step][1:])
+        o = land[0, z].astype(jnp.float32) * share_of[z]
+        o = o + land[1, z].astype(jnp.float32) * share_of[HEADS + z]
         row = jnp.concatenate([o[8 * g : 8 * g + 8] for g in range(GROUP)], axis=1)
-        out_ref[:, z * GROUP * HEAD : (z + 1) * GROUP * HEAD] = row.astype(jnp.bfloat16)
+        start = pl.multiple_of(z * GROUP * HEAD, GROUP * HEAD)
+        out_ref[:, pl.ds(start, GROUP * HEAD)] = row.astype(jnp.bfloat16)
 
     q_copy.wait_send()
-    for group in [*ahead.values(), *right, *left, *turn_right, *turn_left, *core[0], *core[1], *core[2], *core[3], *outs.values()]:
+    for group in [*ahead.values(), *right, *left, turn_right, turn_left, *turn_keys.values(), *turn_values.values(), *core[0], *core[1], *core[2], *core[3], *outs.values()]:
         for copy in group:
             copy.wait_send()
 
@@ -337,9 +359,11 @@
             pltpu.VMEM((2, HEADS, SUF, HEAD), bf16),
             pltpu.VMEM((2, HEADS, 8, HEAD), f32),
             pltpu.VMEM((2, HEADS, 8, HEAD), f32),
+            pltpu.VMEM((COLS, HEAD), f32),
+            pltpu.VMEM((2 * HEADS, SUF, HEAD), f32),
             pltpu.VMEM((HEAD, 2 * HEADS), f32),
             dma((6,)), dma((6,)), dma((24,)), dma((24,)), dma((16,)), dma((16,)),
-            dma, dma, dma((30,)), dma((30,)), dma((5,)), pltpu.SemaphoreType.REGULAR((3,)),
+            dma, dma, dma((30,)), dma((30,)), dma((5,)), pltpu.SemaphoreType.REGULAR((1,)),
         ],
         compiler_params=pltpu.CompilerParams(
             collective_id=0, has_side_effects=True, vmem_limit_bytes=LIMIT

time: 65 us -> 62.4 us (0.960)
  the two profiles are of different devices: /device:TPU:32 before, /device:TPU:6 now
where the time goes in v3:
time: 62.4 us; the launch traced here: 62.2 us
  Pallas kernels  60.7 us (97%)
  local copies, waits for them, and re-layouts  1.57 us (3%)
    pallas_call x1, Pallas kernels, per_device(): pl.pallas_call(kernel, out_shape=jax.ShapeDtypeStruct((SUF // HEADS, HEAD...  60.7 us
    unnamed x1, local copies, waits for them, and re-layouts  1.57 us

profile of v3, /device:TPU:6, one launch (start us, length us, event | category | flops | bytes accessed | tf_op | source)
XLA Modules:
  0.0 62.2 jit_solution(3857896137985233768)
XLA Ops:
  0.0 60.7 %shard_map.73 = bf16[8,8192]{1,0:T(8,128)(2,1)} custom-call(bf16[64,1024]{1,0:T(8,128)(2,1)} %q_ref.1, bf16[64,128]{1,0:T(8,128)(2,1)} %sk_ref.1, bf16[64,128]{1,0:T(8,128)(2,1)} %sv_ref.1, bf16[320,128]{1,0:T(8,128)(2,1)} %pk_ref.1, bf16[320,128]{1,0:T(8,128)(2,1)} %pv_ref.1, s32[64]{0:T(128)} %count_ref.1, s32[64]{0:T(128)} %span_ref.1), custom_call_target="tpu_custom_call" | custom-call | tf_op jit(solution)/shard_map/pallas_call | solution.py:342
  60.7 1.6 %copy.9 = bf16[8,8192]{1,0:T(8,128)(2,1)} copy(bf16[8,8192]{1,0:T(8,128)(2,1)} %shard_map.73) | data formatting | bytes 262144

commit v4 on v3

--- a/solution.py
+++ b/solution.py
@@ -130,6 +130,8 @@
     vbuf[0, 0, 0:HEAD, 0:KEYS] = rows.T.astype(jnp.bfloat16)
 
     pl.semaphore_wait(barrier, len(greeted))
+    for step in (4, 12):
+        pl.semaphore_signal(reach.at[0], inc=1, device_id=along(step), device_id_type=MESH)
 
     def keys_at(slot, piece):
         return kbuf.at[slot, piece // 2, pl.ds(piece % 2 * KEYS, KEYS)]
@@ -163,10 +165,7 @@
     turn_values = {r: [forward(4, 6, r, 8 + r, s_line, r_line, second(3))[1]] for r in (1, 2)}
     q_copy = remote(qown, qraw, s_q, r_q, across)
     begin(ahead[1], ahead[3], right[0], left[0], ahead[2])
-    for n, k in enumerate((4,)):
-        for step in (k, 16 - k):
-            pl.semaphore_signal(reach.at[n], inc=1, device_id=along(step), device_id_type=MESH)
-        pl.semaphore_wait(reach.at[n], 2)
+    pl.semaphore_wait(reach.at[0], 2)
     q_copy.start()
     qbuf[0] = arrange(qown[...])
 
@@ -206,6 +205,11 @@
 
     def sweep(count, pick, queries):
         scores(*pick(0, 0), 0, queries)
+        if count == 1:
+            scores(*pick(0, 1), 1, queries)
+            absorb(*pick(0, 0), 0, queries)
+            absorb(*pick(0, 1), 1, queries)
+            return
 
         def pair(i, carry):
             later = jnp.minimum(i + 1, count - 1)
@@ -341,7 +345,7 @@
     bf16, f32 = jnp.bfloat16, jnp.float32
     return pl.pallas_call(
         kernel,
-        out_shape=jax.ShapeDtypeStruct((SUF // HEADS, HEADS * GROUP * HEAD), bf16),
+        out_shape=pltpu.VMEM((SUF // HEADS, HEADS * GROUP * HEAD), bf16),
         in_specs=[stays] * 5 + [smem] * 2,
         out_specs=vmem,
         scratch_shapes=[

time: 62.4 us -> 60.6 us (0.971)
  Pallas kernels: 60.7 us -> 59.7 us
  local copies, waits for them, and re-layouts: 1.57 us -> 0.66 us
    pallas_call x1, Pallas kernels: 60.7 us -> 59.7 us  [per_device(): pl.pallas_call(kernel, out_shape=pltpu.VMEM((SUF // HEADS, HEADS * GROUP...]
    unnamed x1, local copies, waits for them, and re-layouts: 1.57 us -> 0.66 us
where the time goes in v4:
time: 60.6 us; the launch traced here: 60.4 us
  Pallas kernels  59.7 us (99%)
  local copies, waits for them, and re-layouts  0.66 us (1%)
    pallas_call x1, Pallas kernels, per_device(): pl.pallas_call(kernel, out_shape=pltpu.VMEM((SUF // HEADS, HEADS * GROUP...  59.7 us

profile of v4, /device:TPU:6, one launch (start us, length us, event | category | flops | bytes accessed | tf_op | source)
XLA Modules:
  0.0 60.4 jit_solution(16731293389417822489)
XLA Ops:
  0.0 59.7 %shard_map.73 = bf16[8,8192]{1,0:T(8,128)(2,1)S(1)} custom-call(bf16[64,1024]{1,0:T(8,128)(2,1)} %q_ref.1, bf16[64,128]{1,0:T(8,128)(2,1)} %sk_ref.1, bf16[64,128]{1,0:T(8,128)(2,1)} %sv_ref.1, bf16[320,128]{1,0:T(8,128)(2,1)} %pk_ref.1, bf16[320,128]{1,0:T(8,128)(2,1)} %pv_ref.1, s32[64]{0:T(128)} %count_ref.1, s32[64]{0:T(128)} %span_ref.1), custom_call_target="tpu_custom_call" | custom-call | tf_op jit(solution)/shard_map/pallas_call | solution.py:346
  59.7 0.7 %copy.9 = bf16[8,8192]{1,0:T(8,128)(2,1)} copy(bf16[8,8192]{1,0:T(8,128)(2,1)S(1)} %shard_map.73) | data formatting | bytes 262144

commit v5 on v4

--- a/solution.py
+++ b/solution.py
@@ -264,7 +264,6 @@
     arrived(right[2][1:], right[3])
     begin(core[1][1])
     arrived(core[1][0], core[2][0])
-    sweep(1, lambda i, j: (3 + 2 * j, 0), 0)
     q_copy.wait_recv()
     qbuf[1] = arrange(qraw[...])
     sweep(2, lambda i, j: (i, j), 1)
@@ -301,6 +300,7 @@
             remote(send.at[flip, to], land.at[flip, zl], s_out.at[15 + n], r_out.at[15 + n], who),
         ]
     finish(1, (4, 3, 5, 2, 6, 1, 7, 0))
+    sweep(1, lambda i, j: (3 + 2 * j, 0), 0)
     sweep(2, lambda i, j: (2 + 2 * i + j, 1), 0)
     sweep(2, lambda i, j: (6 + i, j), 0)
     finish(0, (4, 3, 5, 2, 6, 1, 7))

time: 60.6 us -> 60.5 us (level)
  no operation moved by 1% of the time
where the time goes in v5:
time: 60.5 us; the launch traced here: 60.1 us
  Pallas kernels  59.4 us (98%)
  local copies, waits for them, and re-layouts  0.66 us (1%)
    pallas_call x1, Pallas kernels, per_device(): pl.pallas_call(kernel, out_shape=pltpu.VMEM((SUF // HEADS, HEADS * GROUP...  59.4 us

profile of v5, /device:TPU:6, one launch (start us, length us, event | category | flops | bytes accessed | tf_op | source)
XLA Modules:
  0.0 60.1 jit_solution(2611615040624078507)
XLA Ops:
  0.0 59.4 %shard_map.73 = bf16[8,8192]{1,0:T(8,128)(2,1)S(1)} custom-call(bf16[64,1024]{1,0:T(8,128)(2,1)} %q_ref.1, bf16[64,128]{1,0:T(8,128)(2,1)} %sk_ref.1, bf16[64,128]{1,0:T(8,128)(2,1)} %sv_ref.1, bf16[320,128]{1,0:T(8,128)(2,1)} %pk_ref.1, bf16[320,128]{1,0:T(8,128)(2,1)} %pv_ref.1, s32[64]{0:T(128)} %count_ref.1, s32[64]{0:T(128)} %span_ref.1), custom_call_target="tpu_custom_call" | custom-call | tf_op jit(solution)/shard_map/pallas_call | solution.py:346
  59.4 0.7 %copy.9 = bf16[8,8192]{1,0:T(8,128)(2,1)} copy(bf16[8,8192]{1,0:T(8,128)(2,1)S(1)} %shard_map.73) | data formatting | bytes 262144
